TPU v7x, 256 devices: a whole 4x4x8 slice. The times are simulated.
256 devices in a mesh: dp: 32 (over x, z_hi, core), tensor: 8 (over y, z_lo).
Axes of the slice: x: 4, y: 4, z: 8 (z_hi: 4, z_lo: 2; z = z_hi * 2 + z_lo), core: 2. Of those that a mesh axis runs over, the one named last changes fastest.
Arguments:
- tokens: bfloat16 [8192, 6144], P('dp', 'tensor'), may hold values from -6 to 6
- attended: bfloat16 [8192, 48, 128], P('dp', 'tensor'), may hold values from -6 to 6
- out_weight: bfloat16 [128, 48, 6144], P(None, 'tensor'), may hold values from -0.078125 to 0.078125
- cotangent: bfloat16 [8192, 6144], P('dp', 'tensor'), may hold values from -6 to 6
Outputs:
- mixed: bfloat16 [8192, 6144], P('dp', 'tensor')
- grad_attended: bfloat16 [8192, 48, 128], P('dp', 'tensor')
- weight_grad: float32 [128, 48, 6144], P('dp', 'tensor')
All inputs are finite; a program needn't handle non-finite values.
Results may differ from a plain program's by a relative error of at most 0.018.
Values may be sent and summed in bfloat16 or wider, within the bound.
A program may use at most 256 MiB of HBM per device.

v0:
```python
import math

import jax
import jax.numpy as jnp
from jax import lax
from jax.sharding import PartitionSpec as P


def body(tokens, attended, out_weight, cotangent):
    token_count = attended.shape[0]
    data_devices = lax.axis_size("dp")
    partial_value = jnp.einsum(
        "the,ehd->td", attended, out_weight, preferred_element_type=jnp.float32
    )
    own_sum = lax.psum_scatter(
        partial_value.astype(jnp.bfloat16), "tensor", scatter_dimension=1, tiled=True
    ).astype(jnp.float32)
    mixed = (tokens.astype(jnp.float32) + own_sum).astype(jnp.bfloat16)
    whole_grad = lax.all_gather(cotangent, "tensor", axis=1, tiled=True)
    grad_attended = jnp.einsum(
        "td,ehd->the", whole_grad, out_weight, preferred_element_type=jnp.float32
    ).astype(jnp.bfloat16)
    factor = 1.0 / math.sqrt(token_count * data_devices)
    term = (
        jnp.einsum("the,td->ehd", attended, whole_grad, preferred_element_type=jnp.float32) * factor
    )
    weight_grad = lax.psum_scatter(
        term.astype(jnp.bfloat16), "dp", scatter_dimension=0, tiled=True
    ).astype(jnp.float32)
    return (mixed, grad_attended, weight_grad)


def solution(mesh):
    placed = (
        P("dp", "tensor"),
        P("dp", "tensor", None),
        P(None, "tensor", None),
        P("dp", "tensor"),
    )
    return jax.shard_map(
        body,
        mesh=mesh,
        in_specs=placed,
        out_specs=(P("dp", "tensor"), P("dp", "tensor", None), P("dp", "tensor", None)),
        check_vma=False,
    )
```

profile of v0, /device:TPU:1, one launch (start us, length us, event | category | flops | bytes accessed | tf_op | source)
XLA Modules:
  0.0 317.8 jit_solution(1519712126405703991)
XLA Ops:
  7.2 0.0 copy-start
  7.2 0.0 all-gather.2.cloned.1.call-start
  7.2 0.7 all-gather.2.cloned.1.call-update
  7.9 0.0 reduce-scatter.3.cloned.1.call-start
  8.0 0.2 copy-done
  8.2 7.6 %fusion.1 = bf16[256,6144]{1,0:T(8,128)(2,1)} fusion(bf16[256,6,128]{2,0,1:T(8,128)(2,1)S(1)} %copy-done, bf16[128,6,6144]{2,0,1:T(8,128)(2,1)} %param.6), kind=kOutput, calls=%fused_computation.3 | convolution fusion | flops 2417491968 | bytes 12976128 | tf_op jit(solution)/shard_map/the,ehd->td/dot_general | solution.py:12
  15.8 0.0 reduce-scatter.3.cloned.1.call-update
  15.8 0.0 reduce-scatter.5.cloned.1.call-start
  15.9 71.6 %all-gather.2.cloned.1.call-done = bf16[256,6144]{1,0:T(8,128)(2,1)} async-done(((bf16[256,768]{1,0:T(8,128)(2,1)}), bf16[256,6144]{1,0:T(8,128)(2,1)}) %all-gather.2.cloned.1.call-update) | async-done | bytes 3145744 | tf_op jit(solution)/shard_map/all_gather | solution.py:19
  87.5 8.3 %fusion = bf16[128,6,6144]{0,2,1:T(8,128)(2,1)} fusion(bf16[256,6,128]{2,0,1:T(8,128)(2,1)S(1)} %copy-done, bf16[256,6144]{1,0:T(8,128)(2,1)} %all-gather.2.cloned.1.call-done), kind=kOutput, calls=%fused_computation.1 | convolution fusion | flops 2425356288 | bytes 12976128 | tf_op jit(solution)/shard_map/the,td->ehd/dot_general | solution.py:25
  95.8 16.1 %copy.11 = bf16[128,6,6144]{2,1,0:T(8,128)(2,1)} copy(bf16[128,6,6144]{0,2,1:T(8,128)(2,1)} %fusion) | data formatting | bytes 18874368 | tf_op jit(solution)/shard_map/convert_element_type | solution.py:28
  111.9 0.0 reduce-scatter.5.cloned.1.call-update
  111.9 0.0 copy-start.1
  111.9 7.3 %fusion.8 = bf16[256,6,128]{0,2,1:T(8,128)(2,1)S(1)} fusion(bf16[128,6,6144]{2,0,1:T(8,128)(2,1)} %param.6, bf16[256,6144]{1,0:T(8,128)(2,1)} %all-gather.2.cloned.1.call-done), kind=kOutput, calls=%fused_computation.8 | convolution fusion | flops 2416115712 | bytes 12976128 | tf_op jit(solution)/shard_map/td,ehd->the/dot_general | solution.py:20
  119.2 0.9 copy.12
  120.2 44.0 %reduce-scatter.3.cloned.1.call-done = bf16[256,768]{1,0:T(8,128)(2,1)} async-done(((bf16[256,6144]{1,0:T(8,128)(2,1)}), bf16[256,768]{1,0:T(8,128)(2,1)}) %reduce-scatter.3.cloned.1.call-update) | async-done | bytes 393232 | tf_op jit(solution)/shard_map/reduce_scatter | solution.py:15
  164.1 0.0 copy-done.1
  164.1 1.8 add_convert_fusion
  166.0 143.2 %reduce-scatter.5.cloned.1.call-done = bf16[4,6,6144]{2,1,0:T(8,128)(2,1)} async-done(((bf16[128,6,6144]{2,1,0:T(8,128)(2,1)}), bf16[4,6,6144]{2,1,0:T(8,128)(2,1)}) %reduce-scatter.5.cloned.1.call-update) | async-done | bytes 294928 | tf_op jit(solution)/shard_map/reduce_scatter | solution.py:27
  309.2 2.0 copy.13
Async XLA Ops:
  7.2 1.0 copy-start
  7.2 80.3 %all-gather.2.cloned.1.call-start = ((), (), s32[]{:S(2)}) async-start(), calls=%async_computation.3 | async-start | bytes 3538944 | tf_op jit(solution)/shard_map/all_gather | solution.py:19
  7.9 156.2 %reduce-scatter.3.cloned.1.call-start = ((), (), s32[]{:S(2)}) async-start(), calls=%async_computation.2 | async-start | bytes 3538944 | tf_op jit(solution)/shard_map/reduce_scatter | solution.py:15
  15.8 293.4 %reduce-scatter.5.cloned.1.call-start = ((), (), s32[]{:S(2)}) async-start(), calls=%async_computation.4 | async-start | bytes 12976128 | tf_op jit(solution)/shard_map/reduce_scatter | solution.py:27
  111.9 52.3 %copy-start.1 = (bf16[256,768]{1,0:T(8,128)(2,1)S(1)}, bf16[256,768]{1,0:T(8,128)(2,1)}, u32[]{:S(2)}) copy-start(bf16[256,768]{1,0:T(8,128)(2,1)} %param.4) | copy-start | bytes 1179652
Sparse Core Ops, SparseCore 0:
  9.8 77.5 all-gather.1
  90.0 74.0 reduce-scatter.2
  168.3 140.8 reduce-scatter.4
where the time goes:
time: 319 us; the launch traced here: 318 us
  waiting for transfers between devices  259 us (81%)
  matrix products  23.3 us (7%)
  local copies, waits for them, and re-layouts  19.2 us (6%)
  between operations  13.8 us (4%)
    reduce_scatter x1, waiting for transfers between devices, body(): lax.psum_scatter(term.astype(jnp.bfloat16), 'dp', scatter_dimension=0, ti...  143 us
    all_gather x1, waiting for transfers between devices, body(): whole_grad = lax.all_gather(cotangent, 'tensor', axis=1, tiled=True)  71.6 us
    reduce_scatter x1, waiting for transfers between devices, body(): lax.psum_scatter(partial_value.astype(jnp.bfloat16), 'tensor', scatter_di...  44 us
    convert_element_type x1, local copies, waits for them, and re-layouts, body(): term.astype(jnp.bfloat16)  16.1 us
    dot_general x1, matrix products, body(): jnp.einsum('the,td->ehd', attended, whole_grad, preferred_element_type=jn...  8.34 us
    dot_general x1, matrix products, body(): jnp.einsum('the,ehd->td', attended, out_weight, preferred_element_type=jn...  7.64 us
    dot_general x1, matrix products, body(): jnp.einsum('td,ehd->the', whole_grad, out_weight, preferred_element_type=...  7.33 us
  transfers between devices with their start and end apart: 3, of which 3 were waited for; matrix products, arithmetic and copies ran while one was open for 13% of the time, Pallas kernels for 0%

commit v1 on v0

v1 whole, which is shorter than its diff:
```python
import functools
import math

import jax
import jax.numpy as jnp
from jax import lax
from jax.experimental import pallas as pl
from jax.experimental.pallas import tpu as pltpu
from jax.sharding import PartitionSpec as P

MESH = pl.DeviceIdType.MESH
F32 = jnp.float32
BF16 = jnp.bfloat16

Y_OFF = (0, 0, 3, 1, 3, 1, 2, 2)
Z_OFF = (0, 1, 0, 0, 1, 1, 0, 1)
ORDER = (0, 1, 2, 3, 6, 4, 5, 7)
T = 256
E = 768
H = 384


def nt(a, b):
    return lax.dot_general(a, b, (((1,), (1,)), ((), ())), preferred_element_type=F32)


def nn(a, b):
    return lax.dot_general(a, b, (((1,), (0,)), ((), ())), preferred_element_type=F32)


def kernel(
    factor,
    tok_hbm, att_hbm, w_hbm, cot_hbm,
    mixed_hbm, gatt_hbm, wg_hbm,
    tok, a_own, a_oth, perm, at_own, at_oth, w, cot, cotx, part,
    br, bfin, bz, gacc, gout,
    term, xr, xfin, xs, zr, zfin, res, resx,
    lsem, osem, ssem, rsem,
):
    dp, tp = lax.axis_index("dp"), lax.axis_index("tensor")
    x, zh, c = dp // 8, (dp // 2) % 4, dp % 2
    y, zl = tp // 2, tp % 2

    def dev(x_, zh_, c_, y_, zl_):
        return ((x_ * 4 + zh_) * 2 + c_, y_ * 2 + zl_)

    xp, xm = dev((x + 1) % 4, zh, c, y, zl), dev((x + 3) % 4, zh, c, y, zl)
    yp, ym = dev(x, zh, c, (y + 1) % 4, zl), dev(x, zh, c, (y + 3) % 4, zl)
    zp, zm = dev(x, (zh + 1) % 4, c, y, zl), dev(x, (zh + 3) % 4, c, y, zl)
    zo, co = dev(x, zh, c, y, 1 - zl), dev(x, zh, 1 - c, y, zl)

    barrier = pltpu.get_barrier_semaphore()
    for to in (xp, xm, yp, ym, zp, zm, zo, co):
        pl.semaphore_signal(barrier, inc=1, device_id=to, device_id_type=MESH)

    def block(s):
        return ((y + Y_OFF[s]) % 4) * 2 + (zl + Z_OFF[s]) % 2

    count = [0]

    def load(src, dst):
        copy = pltpu.make_async_copy(src, dst, lsem.at[count[0]])
        count[0] += 1
        copy.start()
        return copy

    l_cot = [load(cot_hbm.at[:, pl.ds(H * h, H)], cot.at[0, h]) for h in range(2)]
    l_att = [load(att_hbm.at[h], a_own.at[:, pl.ds(128 * h, 128)]) for h in range(6)]
    l_w = {}
    for s in (7, 5, 4, 1, 6, 3, 2, 0):
        for h in range(2):
            col = pl.multiple_of(block(s) * E + H * h, 128)
            l_w[s, h] = load(w_hbm.at[:, pl.ds(col, H)], w.at[s, h])
    l_tok = load(tok_hbm, tok)

    sent = []

    def send(src, dst, to):
        i = len(sent)
        copy = pltpu.make_async_remote_copy(
            src_ref=src, dst_ref=dst, send_sem=ssem.at[i], recv_sem=rsem.at[i],
            device_id=to, device_id_type=MESH,
        )
        copy.start()
        sent.append(copy)
        return copy

    outs = []

    def store(src, dst):
        copy = pltpu.make_async_copy(src, dst, osem.at[len(outs)])
        copy.start()
        outs.append(copy)

    def make_perm(i, _):
        row = lax.broadcasted_iota(jnp.int32, (48, E), 0)
        col = lax.broadcasted_iota(jnp.int32, (48, E), 1)
        core = (row >= 24).astype(jnp.int32)
        r = row - 24 * core
        want = (r >> 2) * 128 + 8 * i + 4 * core + (r & 3)
        perm[i // 4, pl.ds(pl.multiple_of((i % 4) * 48, 16), 48), :] = (
            (col == want).astype(F32).astype(BF16)
        )
        return 0

    def permute(src, dst):
        def go(i, _):
            dst[i] = nt(perm[i], src[...]).astype(BF16)
            return 0

        lax.fori_loop(0, 4, go, 0)

    a = {}
    cx = {}

    def core_send(s):
        cx[s] = send(cot.at[s, 1 - c], cotx.at[s], co)

    pl.semaphore_wait(barrier, 8)
    for h in range(2):
        l_cot[h].wait()
    a[2, 0] = send(cot.at[0, 0], cot.at[2, 0], yp)
    a[3, 1] = send(cot.at[0, 1], cot.at[3, 1], ym)
    a[1, 0] = send(cot.at[0, 0], cot.at[1, 0], zo)
    core_send(0)
    a[2, 1] = send(cot.at[0, 1], cot.at[2, 1], yp)
    a[3, 0] = send(cot.at[0, 0], cot.at[3, 0], ym)
    a[1, 1] = send(cot.at[0, 1], cot.at[1, 1], zo)
    for cp in l_att:
        cp.wait()
    a_swap = send(a_own, a_oth, co)
    lax.fori_loop(0, 16, make_perm, 0)
    permute(a_own, at_own)
    a_swap.wait_recv()
    permute(a_oth, at_oth)

    x1, x2, z1, z2, r1 = {}, {}, {}, {}, {}

    def c_term(s):
        cx[s].wait_recv()

        def go(i, _):
            val = nn(at_own[i], cot[s, c]) + nn(at_oth[i], cotx[s])
            term[s, i] = val.astype(BF16).reshape(4, 48, H)
            return 0

        lax.fori_loop(0, 4, go, 0)
        xf, xn, xl = (x + 2) % 4, (x + 1) % 4, (x + 3) % 4
        x1[s] = [
            send(term.at[s, xf, pl.ds(0, 2)], xr.at[s, 0], xp),
            send(term.at[s, xf, pl.ds(2, 2)], xr.at[s, 1], xm),
            send(term.at[s, xn, pl.ds(2, 2)], xfin.at[s, 0, pl.ds(2, 2)], xp),
            send(term.at[s, xl, pl.ds(0, 2)], xfin.at[s, 1, pl.ds(0, 2)], xm),
        ]

    def c_relay(s):
        xn, xl = (x + 1) % 4, (x + 3) % 4
        x2[s] = []
        x1[s][0].wait_recv()
        t = term[s, xn, pl.ds(0, 2)].astype(F32) + xr[s, 0].astype(F32)
        term[s, xn, pl.ds(0, 2)] = t.astype(BF16)
        x2[s].append(send(term.at[s, xn, pl.ds(0, 2)], xfin.at[s, 0, pl.ds(0, 2)], xp))
        x1[s][1].wait_recv()
        t = term[s, xl, pl.ds(2, 2)].astype(F32) + xr[s, 1].astype(F32)
        term[s, xl, pl.ds(2, 2)] = t.astype(BF16)
        x2[s].append(send(term.at[s, xl, pl.ds(2, 2)], xfin.at[s, 1, pl.ds(2, 2)], xm))

    def z_places(s):
        even = ORDER.index(s) % 2 == 0
        up, down = (zh + 1) % 4, (zh + 3) % 4
        return (up, down, zp, zm) if even else (down, up, zm, zp)

    def c_xsum(s):
        x1[s][2].wait_recv()
        x1[s][3].wait_recv()
        x2[s][0].wait_recv()
        x2[s][1].wait_recv()
        t = term[s, x].astype(F32) + xfin[s, 0].astype(F32) + xfin[s, 1].astype(F32)
        xs[s] = t.astype(BF16)
        _, n_m, to_p, to_m = z_places(s)
        z1[s] = [
            send(xs.at[s, (zh + 2) % 4], zr.at[s], to_p),
            send(xs.at[s, n_m], zfin.at[s, 1], to_m),
        ]

    def c_zrelay(s):
        n_p, _, to_p, _ = z_places(s)
        z1[s][0].wait_recv()
        t = xs[s, n_p].astype(F32) + zr[s].astype(F32)
        xs[s, n_p] = t.astype(BF16)
        z2[s] = send(xs.at[s, n_p], zfin.at[s, 0], to_p)

    def c_zsum(s):
        z1[s][1].wait_recv()
        z2[s].wait_recv()
        t = xs[s, zh].astype(F32) + zfin[s, 0].astype(F32) + zfin[s, 1].astype(F32)
        res[s] = (t * factor).reshape(2, 24, H)
        r1[s] = send(res.at[s, 1 - c], resx.at[s], co)
        col = pl.multiple_of(block(s) * E + H * c, 128)
        store(res.at[s, c], wg_hbm.at[:, pl.ds(col, H)])

    def c_out(s):
        r1[s].wait_recv()
        col = pl.multiple_of(block(s) * E + H * (1 - c), 128)
        store(resx.at[s], wg_hbm.at[:, pl.ds(col, H)])

    def grad(s):
        def go(h, _):
            gacc[...] += nt(cot[s, h], w[s, h])
            return 0

        lax.fori_loop(0, 2, go, 0)

    def b_part(s):
        for h in range(2):
            l_w[s, h].wait()

        def go(h, _):
            part[s, h] = nn(a_own[...], w[s, h]).astype(BF16)
            return 0

        lax.fori_loop(0, 2, go, 0)

    ROUND = ((7, 5, 4, 1), (6, 3, 2, 0))
    b1, b2, b3 = {}, {}, {}

    def b_send(r):
        f, n, m, _ = ROUND[r]
        b1[r] = [
            send(part.at[f, 0], br.at[r, 0], yp),
            send(part.at[f, 1], br.at[r, 1], ym),
            send(part.at[n, 1], bfin.at[r, 0, 1], yp),
            send(part.at[m, 0], bfin.at[r, 1, 0], ym),
        ]

    def b_relay(r):
        _, n, m, _ = ROUND[r]
        b1[r][0].wait_recv()
        part[n, 0] = (part[n, 0].astype(F32) + br[r, 0].astype(F32)).astype(BF16)
        b2[r] = [send(part.at[n, 0], bfin.at[r, 0, 0], yp)]
        b1[r][1].wait_recv()
        part[m, 1] = (part[m, 1].astype(F32) + br[r, 1].astype(F32)).astype(BF16)
        b2[r].append(send(part.at[m, 1], bfin.at[r, 1, 1], ym))

    def b_sum(r, h):
        o = ROUND[r][3]
        return part[o, h].astype(F32) + bfin[r, 0, h].astype(F32) + bfin[r, 1, h].astype(F32)

    def b_wait(r):
        b1[r][2].wait_recv()
        b1[r][3].wait_recv()
        b2[r][0].wait_recv()
        b2[r][1].wait_recv()

    def b_cross():
        b_wait(0)
        for h in range(2):
            part[1, h] = b_sum(0, h).astype(BF16)
            b3[h] = send(part.at[1, h], bz.at[h], zo)

    def b_mix():
        b_wait(1)
        l_tok.wait()
        for h in range(2):
            b3[h].wait_recv()
            t = b_sum(1, h) + bz[h].astype(F32)
            tok[:, pl.ds(H * h, H)] = (tok[:, pl.ds(H * h, H)].astype(F32) + t).astype(BF16)
        store(tok, mixed_hbm)

    gacc[...] = jnp.zeros_like(gacc)
    c_term(0)
    a[2, 0].wait_recv()
    a[6, 0] = send(cot.at[2, 0], cot.at[6, 0], yp)
    a[3, 1].wait_recv()
    a[6, 1] = send(cot.at[3, 1], cot.at[6, 1], ym)
    c_relay(0)
    b_part(7)
    b_part(5)
    b_part(4)
    a[1, 0].wait_recv()
    a[1, 1].wait_recv()
    a[4, 0] = send(cot.at[1, 0], cot.at[4, 0], yp)
    a[5, 1] = send(cot.at[1, 1], cot.at[5, 1], ym)
    a[4, 1] = send(cot.at[1, 1], cot.at[4, 1], yp)
    a[5, 0] = send(cot.at[1, 0], cot.at[5, 0], ym)
    core_send(1)
    a[2, 1].wait_recv()
    core_send(2)
    a[3, 0].wait_recv()
    core_send(3)
    c_term(1)
    c_xsum(0)
    c_term(2)
    c_relay(1)
    c_zrelay(0)
    a[6, 0].wait_recv()
    a[6, 1].wait_recv()
    a[7, 0] = send(cot.at[6, 0], cot.at[7, 0], zo)
    a[7, 1] = send(cot.at[6, 1], cot.at[7, 1], zo)
    core_send(6)
    b_send(0)
    c_term(3)
    c_relay(2)
    c_xsum(1)
    c_zsum(0)
    b_part(1)
    b_part(6)
    b_part(3)
    b_part(2)
    b_part(0)
    c_term(6)
    c_relay(3)
    c_xsum(2)
    c_zrelay(1)
    for s in (0, 1, 2, 3, 6):
        grad(s)
    for s in (4, 5):
        a[s, 0].wait_recv()
        a[s, 1].wait_recv()
        core_send(s)
    c_term(4)
    c_relay(6)
    c_xsum(3)
    c_zrelay(2)
    c_zsum(1)
    b_relay(0)
    b_send(1)
    c_term(5)
    c_relay(4)
    c_xsum(6)
    c_zrelay(3)
    c_zsum(2)
    a[7, 0].wait_recv()
    a[7, 1].wait_recv()
    core_send(7)
    c_term(7)
    c_relay(5)
    c_xsum(4)
    c_zrelay(6)
    c_zsum(3)
    b_cross()
    c_relay(7)
    c_xsum(5)
    c_zrelay(4)
    c_zsum(6)
    b_relay(1)
    for s in (4, 5, 7):
        grad(s)
    for h in range(6):
        gout[h] = gacc[:, pl.ds(128 * h, 128)].astype(BF16)
    store(gout, gatt_hbm)
    c_xsum(7)
    c_zrelay(5)
    c_zsum(4)
    c_zrelay(7)
    c_zsum(5)
    for s in (0, 1, 2, 3, 6, 4):
        c_out(s)
    b_mix()
    c_zsum(7)
    c_out(5)
    c_out(7)
    for cp in sent:
        cp.wait_send()
    for cp in outs:
        cp.wait()


N_SEND = 128


def body(tokens, attended, out_weight, cotangent):
    factor = 1.0 / math.sqrt(attended.shape[0] * lax.axis_size("dp"))
    any_spec = pl.BlockSpec(memory_space=pl.ANY)
    vm = pltpu.VMEM
    mixed, gatt, wg = pl.pallas_call(
        functools.partial(kernel, factor),
        out_shape=(
            jax.ShapeDtypeStruct((T, E), BF16),
            jax.ShapeDtypeStruct((6, T, 128), BF16),
            jax.ShapeDtypeStruct((24, 8 * E), F32),
        ),
        in_specs=[any_spec] * 4,
        out_specs=(any_spec,) * 3,
        scratch_shapes=[
            vm((T, E), BF16),
            vm((T, E), BF16),
            vm((T, E), BF16),
            vm((4, 192, E), BF16),
            vm((4, 192, T), BF16),
            vm((4, 192, T), BF16),
            vm((8, 2, E, H), BF16),
            vm((8, 2, T, H), BF16),
            vm((8, T, H), BF16),
            vm((8, 2, T, H), BF16),
            vm((2, 2, T, H), BF16),
            vm((2, 2, 2, T, H), BF16),
            vm((2, T, H), BF16),
            vm((T, E), F32),
            vm((6, T, 128), BF16),
            vm((8, 4, 4, 48, H), BF16),
            vm((8, 2, 2, 48, H), BF16),
            vm((8, 2, 4, 48, H), BF16),
            vm((8, 4, 48, H), BF16),
            vm((8, 48, H), BF16),
            vm((8, 2, 48, H), BF16),
            vm((8, 2, 24, H), F32),
            vm((8, 24, H), F32),
            pltpu.SemaphoreType.DMA((25,)),
            pltpu.SemaphoreType.DMA((18,)),
            pltpu.SemaphoreType.DMA((N_SEND,)),
            pltpu.SemaphoreType.DMA((N_SEND,)),
        ],
        compiler_params=pltpu.CompilerParams(
            collective_id=0, has_side_effects=True, vmem_limit_bytes=56 * 2**20
        ),
    )(
        tokens,
        jnp.transpose(attended, (1, 0, 2)),
        jnp.transpose(out_weight, (1, 0, 2)).reshape(E, 8 * E),
        cotangent,
    )
    return (
        mixed,
        jnp.transpose(gatt, (1, 0, 2)),
        jnp.transpose(wg.reshape(6, 4, 8 * E), (1, 0, 2)),
    )


def solution(mesh):
    placed = (
        P("dp", "tensor"),
        P("dp", "tensor", None),
        P(None, "tensor", None),
        P("dp", "tensor"),
    )
    return jax.shard_map(
        body,
        mesh=mesh,
        in_specs=placed,
        out_specs=(P("dp", "tensor"), P("dp", "tensor", None), P("dp", "tensor", None)),
        check_vma=False,
    )
```

time: 319 us -> 89 us (0.28)
  waiting for transfers between devices: 259 us -> 0 us
  Pallas kernels: 0 us -> 82.6 us
  matrix products: 23.3 us -> 0 us
  local copies, waits for them, and re-layouts: 19.2 us -> 5.58 us
  between operations: 13.8 us -> 0.64 us
    reduce_scatter x2 -> x0, waiting for transfers between devices: 187 us -> none  [the longest x1 143 us: body(): lax.psum_scatter(term.astype(jnp.bfloat16), 'dp', scatter_dimension=0, ti...]
    pallas_call x0 -> x1, Pallas kernels: none -> 82.6 us  [body(): pl.pallas_call(functools.partial(kernel, factor), out_shape=(jax.ShapeDty...]
    all_gather x1 -> x0, waiting for transfers between devices: 71.6 us -> none  [body(): whole_grad = lax.all_gather(cotangent, 'tensor', axis=1, tiled=True)]
    dot_general x3 -> x0, matrix products: 23.3 us -> none  [the longest x1 8.34 us: body(): jnp.einsum('the,td->ehd', attended, whole_grad, preferred_element_type=jn...]
    convert_element_type x1 -> x0, local copies, waits for them, and re-layouts: 16.1 us -> none  [body(): term.astype(jnp.bfloat16)]
  transfers between devices with their start and end apart: 3 -> 0, of which waited for: 3 -> 0; matrix products, arithmetic and copies ran while one was open for 13% -> 0% of each run, Pallas kernels for 0% -> 0%
where the time goes in v1:
time: 89 us; the launch traced here: 88.8 us
  Pallas kernels  82.6 us (93%)
  local copies, waits for them, and re-layouts  5.58 us (6%)
    pallas_call x1, Pallas kernels, body(): pl.pallas_call(functools.partial(kernel, factor), out_shape=(jax.ShapeDty...  82.6 us
    unnamed x2, local copies, waits for them, and re-layouts  3.53 us
    reshape x1, local copies, waits for them, and re-layouts, body(): wg.reshape(6, 4, 8 * E)  2.05 us

profile of v1, /device:TPU:1, one launch (start us, length us, event | category | flops | bytes accessed | tf_op | source)
XLA Modules:
  0.0 88.8 jit_solution(16558762318889761875)
XLA Ops:
  0.6 82.6 %shard_map.67 = (bf16[256,768]{1,0:T(8,128)(2,1)}, bf16[6,256,128]{2,1,0:T(8,128)(2,1)}, f32[24,6144]{1,0:T(8,128)}) custom-call(bf16[256,768]{1,0:T(8,128)(2,1)} %tok_hbm.1, bf16[6,256,128]{2,1,0:T(8,128)(2,1)} %bitcast.9, bf16[768,6144]{1,0:T(8,128)(2,1)} %bitcast.6, bf16[256,768]{1,0:T(8,128)(2,1)} %cot_hbm.1), custom_call_target="tpu_custom_call" | custom-call | tf_op jit(solution)/shard_map/pallas_call | solution.py:376
  83.2 2.0 %reshape.13 = f32[6,4,6144]{2,1,0:T(4,128)} reshape(f32[24,6144]{1,0:T(8,128)} %get-tuple-element.8) | data formatting | bytes 1179648 | tf_op jit(solution)/shard_map/reshape | solution.py:426
  85.3 1.8 %copy.9 = bf16[256,768]{1,0:T(8,128)(2,1)} copy(bf16[256,768]{1,0:T(8,128)(2,1)} %get-tuple-element.12) | data formatting | bytes 786432
  87.0 1.8 %copy.10 = bf16[256,6,128]{2,0,1:T(8,128)(2,1)} copy(bf16[256,6,128]{2,0,1:T(8,128)(2,1)} %bitcast.8) | data formatting | bytes 786432

commit v2 on v0

v2 whole, which is shorter than its diff:
```python
import functools
import math

import jax
import jax.numpy as jnp
from jax import lax
from jax.experimental import pallas as pl
from jax.experimental.pallas import tpu as pltpu
from jax.sharding import PartitionSpec as P

MESH = pl.DeviceIdType.MESH
F32 = jnp.float32
BF16 = jnp.bfloat16

Y_OFF = (0, 0, 3, 1, 3, 1, 2, 2)
Z_OFF = (0, 1, 0, 0, 1, 1, 0, 1)
T = 256
E = 768
H = 384
DIRECT = ()


def nt(a, b):
    return lax.dot_general(a, b, (((1,), (1,)), ((), ())), preferred_element_type=F32)


def nn(a, b):
    return lax.dot_general(a, b, (((1,), (0,)), ((), ())), preferred_element_type=F32)


def kernel(
    factor,
    tok_hbm, att_hbm, w_hbm, cot_hbm,
    mixed, gatt, wg,
    tok, a_own, perm, at, w, cot, part,
    br, bfin, bz, gacc,
    term, xr, xfin, xs, zr, zfin, res, resx,
    lsem, ssem, rsem,
):
    dp, tp = lax.axis_index("dp"), lax.axis_index("tensor")
    x, zh, c = dp // 8, (dp // 2) % 4, dp % 2
    y, zl = tp // 2, tp % 2

    def dev(x_, zh_, c_, y_, zl_):
        return ((x_ * 4 + zh_) * 2 + c_, y_ * 2 + zl_)

    xp, xm = dev((x + 1) % 4, zh, c, y, zl), dev((x + 3) % 4, zh, c, y, zl)
    yp, ym = dev(x, zh, c, (y + 1) % 4, zl), dev(x, zh, c, (y + 3) % 4, zl)
    zp, zm = dev(x, (zh + 1) % 4, c, y, zl), dev(x, (zh + 3) % 4, c, y, zl)
    z2 = dev(x, (zh + 2) % 4, c, y, zl)
    zo, co = dev(x, zh, c, y, 1 - zl), dev(x, zh, 1 - c, y, zl)

    barrier = pltpu.get_barrier_semaphore()
    for to in (xp, xm, yp, ym, zp, zm, z2, zo, co):
        pl.semaphore_signal(barrier, inc=1, device_id=to, device_id_type=MESH)

    def slot(i, k):
        return (0, 2 + k, 3 - k, 1, 6, 7, 4 + k, 5 - k)[i]

    def block(s):
        return ((y + Y_OFF[s]) % 4) * 2 + (zl + Z_OFF[s]) % 2

    def step_block(i, k):
        yo = (0, 3 - 2 * k, 1 + 2 * k, 0, 2, 2, 3 - 2 * k, 1 + 2 * k)[i]
        return ((y + yo) % 4) * 2 + (zl + (0, 0, 0, 1, 0, 1, 1, 1)[i]) % 2

    count = [0]

    def load(src, dst):
        copy = pltpu.make_async_copy(src, dst, lsem.at[count[0]])
        count[0] += 1
        copy.start()
        return copy

    l_cot = [load(cot_hbm.at[:, pl.ds(H * h, H)], cot.at[0, 1 + h]) for h in range(2)]
    l_att = [load(att_hbm.at[h], a_own.at[:, pl.ds(128 * h, 128)]) for h in range(6)]
    l_w = {}
    for s in (7, 5, 4, 1, 6, 3, 2, 0):
        for h in range(2):
            col = pl.multiple_of(block(s) * E + H * h, 128)
            l_w[s, h] = load(w_hbm.at[:, pl.ds(col, H)], w.at[s, h])
    l_tok = load(tok_hbm, tok)

    sent = []

    def send(src, dst, to):
        i = len(sent)
        copy = pltpu.make_async_remote_copy(
            src_ref=src, dst_ref=dst, send_sem=ssem.at[i], recv_sem=rsem.at[i],
            device_id=to, device_id_type=MESH,
        )
        copy.start()
        sent.append(copy)
        return copy

    a, cx = {}, {}

    def a_send(src, s, h, to):
        a[s, h] = send(cot.at[src, 1 + h], cot.at[s, 1 + h], to)

    def core_send(i):
        s = slot(i, 1 - c)
        cx[i] = send(cot.at[s, 2 - c], cot.at[s, 3 * (1 - c)], co)

    def make_perm(i, _):
        row = lax.broadcasted_iota(jnp.int32, (48, 128), 0)
        core = (row >= 24).astype(jnp.int32)
        r = row - 24 * core
        want = (r >> 2) * 128 + 8 * i + 4 * core + (r & 3)
        want = want - lax.broadcasted_iota(jnp.int32, (48, 128), 1)
        rows = pl.ds(pl.multiple_of((i % 8) * 48, 16), 48)
        for h in range(6):
            perm[i // 8, rows, pl.ds(128 * h, 128)] = (
                jnp.where(want == 128 * h, 1.0, 0.0).astype(BF16)
            )
        return 0

    lax.fori_loop(0, 16, make_perm, 0)
    pl.semaphore_wait(barrier, 9)
    l_cot[0].wait()
    l_cot[1].wait()
    a_send(0, 2, 0, yp)
    a_send(0, 3, 1, ym)
    a_send(0, 1, 0, zo)
    core_send(0)
    a_send(0, 2, 1, yp)
    a_send(0, 3, 0, ym)
    a_send(0, 1, 1, zo)
    for cp in l_att:
        cp.wait()
    mine = pl.ds(pl.multiple_of(T * (1 - c), T), T)

    def permute(i, _):
        at[i, :, mine] = nt(perm[i], a_own[...]).astype(BF16)
        return 0

    lax.fori_loop(0, 2, permute, 0)
    a_swap = send(at.at[:, :, mine], at.at[:, :, mine], co)

    x1, x2, zs, zt, r1 = {}, {}, {}, {}, {}

    def c_term(i):
        cx[i].wait_recv()
        s = slot(i, c)

        val = nn(at[...].reshape(E, 2 * T), cot[s, pl.ds(2 * c, 2)].reshape(2 * T, H))
        term[i] = val.astype(BF16).reshape(4, 4, 48, H)
        xf, xn, xl = (x + 2) % 4, (x + 1) % 4, (x + 3) % 4
        x1[i] = [
            send(term.at[i, xf, pl.ds(0, 2)], xr.at[i, 0], xp),
            send(term.at[i, xf, pl.ds(2, 2)], xr.at[i, 1], xm),
            send(term.at[i, xn, pl.ds(2, 2)], xfin.at[i, 0, pl.ds(2, 2)], xp),
            send(term.at[i, xl, pl.ds(0, 2)], xfin.at[i, 1, pl.ds(0, 2)], xm),
        ]

    def c_relay(i):
        xn, xl = (x + 1) % 4, (x + 3) % 4
        x2[i] = []
        x1[i][0].wait_recv()
        t = term[i, xn, pl.ds(0, 2)].astype(F32) + xr[i, 0].astype(F32)
        term[i, xn, pl.ds(0, 2)] = t.astype(BF16)
        x2[i].append(send(term.at[i, xn, pl.ds(0, 2)], xfin.at[i, 0, pl.ds(0, 2)], xp))
        x1[i][1].wait_recv()
        t = term[i, xl, pl.ds(2, 2)].astype(F32) + xr[i, 1].astype(F32)
        term[i, xl, pl.ds(2, 2)] = t.astype(BF16)
        x2[i].append(send(term.at[i, xl, pl.ds(2, 2)], xfin.at[i, 1, pl.ds(2, 2)], xm))

    def z_places(i):
        up, down = (zh + 1) % 4, (zh + 3) % 4
        return (up, down, zp, zm) if i % 2 == 0 else (down, up, zm, zp)

    def c_xsum(i):
        x1[i][2].wait_recv()
        x1[i][3].wait_recv()
        x2[i][0].wait_recv()
        x2[i][1].wait_recv()
        t = term[i, x].astype(F32) + xfin[i, 0].astype(F32) + xfin[i, 1].astype(F32)
        xs[i] = t.astype(BF16)
        n_p, n_m, to_p, to_m = z_places(i)
        if i in DIRECT:
            zs[i] = send(xs.at[i, (zh + 2) % 4], zr.at[i], z2)
            zt[i] = send(xs.at[i, n_p], zfin.at[i, 0], to_p)
        else:
            zs[i] = send(xs.at[i, (zh + 2) % 4], zr.at[i], to_p)
        zs[i] = zs[i], send(xs.at[i, n_m], zfin.at[i, 1], to_m)

    def c_zrelay(i):
        n_p, _, to_p, _ = z_places(i)
        zs[i][0].wait_recv()
        t = xs[i, n_p].astype(F32) + zr[i].astype(F32)
        xs[i, n_p] = t.astype(BF16)
        zt[i] = send(xs.at[i, n_p], zfin.at[i, 0], to_p)

    def put(val, col):
        cols = pl.ds(pl.multiple_of(col, 128), H)
        for h in range(6):
            wg[h, :, cols] = val[4 * h : 4 * h + 4]

    def c_zsum(i):
        zs[i][1].wait_recv()
        zt[i].wait_recv()
        t = xs[i, zh].astype(F32) + zfin[i, 0].astype(F32) + zfin[i, 1].astype(F32)
        if i in DIRECT:
            zs[i][0].wait_recv()
            t = t + zr[i].astype(F32)
        res[i] = (t * factor).reshape(2, 24, H)
        r1[i] = send(res.at[i, 1 - c], resx.at[i], co)
        put(res[i, c], step_block(i, c) * E + H * c)

    def c_out(i):
        r1[i].wait_recv()
        put(resx[i], step_block(i, 1 - c) * E + H * (1 - c))

    def grad(s):
        def go(b, _):
            cols = pl.ds(pl.multiple_of(b * T, T), T)
            t = nt(cot[s, 1], w[s, 0, cols]) + nt(cot[s, 2], w[s, 1, cols])
            gacc[:, cols] += t
            return 0

        lax.fori_loop(0, 3, go, 0)

    def b_part(s):
        for h in range(2):
            l_w[s, h].wait()

        def go(h, _):
            part[s, h] = nn(a_own[...], w[s, h]).astype(BF16)
            return 0

        lax.fori_loop(0, 2, go, 0)

    ROUND = ((7, 5, 4, 1), (6, 3, 2, 0))
    b1, bn, b2, b3 = {}, {}, {}, {}

    def b_far(r):
        f = ROUND[r][0]
        b1[r] = [
            send(part.at[f, 0], br.at[r, 0], yp),
            send(part.at[f, 1], br.at[r, 1], ym),
        ]

    def b_near(r):
        _, n, m, _ = ROUND[r]
        bn[r] = [
            send(part.at[n, 1], bfin.at[r, 0, 1], yp),
            send(part.at[m, 0], bfin.at[r, 1, 0], ym),
        ]

    def b_relay(r):
        _, n, m, _ = ROUND[r]
        b1[r][0].wait_recv()
        part[n, 0] = (part[n, 0].astype(F32) + br[r, 0].astype(F32)).astype(BF16)
        b2[r] = [send(part.at[n, 0], bfin.at[r, 0, 0], yp)]
        b1[r][1].wait_recv()
        part[m, 1] = (part[m, 1].astype(F32) + br[r, 1].astype(F32)).astype(BF16)
        b2[r].append(send(part.at[m, 1], bfin.at[r, 1, 1], ym))

    def b_sum(r, h):
        o = ROUND[r][3]
        return part[o, h].astype(F32) + bfin[r, 0, h].astype(F32) + bfin[r, 1, h].astype(F32)

    def b_wait(r):
        bn[r][0].wait_recv()
        bn[r][1].wait_recv()
        b2[r][0].wait_recv()
        b2[r][1].wait_recv()

    def b_cross():
        b_wait(0)
        for h in range(2):
            part[1, h] = b_sum(0, h).astype(BF16)
            b3[h] = send(part.at[1, h], bz.at[h], zo)

    def b_mix():
        b_wait(1)
        l_tok.wait()
        for h in range(2):
            b3[h].wait_recv()
            t = b_sum(1, h) + bz[h].astype(F32)
            cols = pl.ds(H * h, H)
            mixed[:, cols] = (tok[:, cols].astype(F32) + t).astype(BF16)

    def grad_out():
        for h in range(6):
            gatt[h] = gacc[:, pl.ds(128 * h, 128)].astype(BF16)

    def arrived(*keys):
        for k in keys:
            a[k].wait_recv()

    a_swap.wait_recv()
    gacc[...] = jnp.zeros_like(gacc)
    b_part(7)
    c_term(0)
    arrived((2, 0), (3, 1))
    a_send(2, 6, 0, yp)
    a_send(3, 6, 1, ym)
    core_send(1)
    b_part(5)
    c_relay(0)
    c_term(1)
    arrived((1, 0), (1, 1))
    core_send(3)
    a_send(1, 4, 0, yp)
    a_send(1, 5, 1, ym)
    b_part(4)
    b_near(0)
    c_term(3)
    c_xsum(0)
    arrived((6, 0), (6, 1))
    a_send(6, 7, 0, zo)
    a_send(6, 7, 1, zo)
    core_send(4)
    b_part(2)
    b_part(0)
    arrived((2, 1), (3, 0))
    core_send(2)
    c_relay(3)
    c_term(4)
    c_zrelay(0)
    c_term(2)
    b_part(3)
    b_far(0)
    a_send(1, 4, 1, yp)
    a_send(1, 5, 0, ym)
    grad(0)
    c_relay(1)
    c_relay(4)
    c_xsum(3)
    arrived((4, 0), (5, 1))
    core_send(6)
    b_part(1)
    c_relay(2)
    c_term(6)
    b_relay(0)
    c_zrelay(3)
    arrived((7, 0), (7, 1))
    core_send(5)
    b_part(6)
    c_xsum(1)
    c_zsum(0)
    c_xsum(4)
    c_out(0)
    b_far(1)
    arrived((4, 1), (5, 0))
    core_send(7)
    c_term(5)
    c_xsum(2)
    c_term(7)
    c_zrelay(4)
    c_zrelay(1)
    b_cross()
    c_zsum(3)
    b_near(1)
    grad(3)
    grad(1)
    c_relay(5)
    c_relay(7)
    b_relay(1)
    grad(5)
    c_zrelay(2)
    grad(6)
    c_relay(6)
    grad(2)
    c_xsum(7)
    c_xsum(5)
    grad(7)
    c_xsum(6)
    c_zsum(1)
    grad(4)
    c_out(1)
    c_zrelay(7)
    b_mix()
    c_zrelay(5)
    c_zsum(2)
    c_zrelay(6)
    c_zsum(4)
    c_zsum(7)
    c_out(2)
    c_out(3)
    c_out(4)
    grad_out()
    c_zsum(5)
    c_zsum(6)
    c_out(7)
    c_out(5)
    c_out(6)
    for cp in sent:
        cp.wait_send()


N_SEND = 120


def body(tokens, attended, out_weight, cotangent):
    factor = 1.0 / math.sqrt(attended.shape[0] * lax.axis_size("dp"))
    any_spec = pl.BlockSpec(memory_space=pl.ANY)
    vm = pltpu.VMEM
    mixed, gatt, wg = pl.pallas_call(
        functools.partial(kernel, factor),
        out_shape=(
            vm((T, E), BF16),
            vm((6, T, 128), BF16),
            vm((6, 4, 8 * E), F32),
        ),
        in_specs=[any_spec] * 4,
        out_specs=(pl.BlockSpec(memory_space=vm),) * 3,
        scratch_shapes=[
            vm((T, E), BF16),
            vm((T, E), BF16),
            vm((2, H, E), BF16),
            vm((2, H, 2 * T), BF16),
            vm((8, 2, E, H), BF16),
            vm((8, 4, T, H), BF16),
            vm((8, 2, T, H), BF16),
            vm((2, 2, T, H), BF16),
            vm((2, 2, 2, T, H), BF16),
            vm((2, T, H), BF16),
            vm((T, E), F32),
            vm((8, 4, 4, 48, H), BF16),
            vm((8, 2, 2, 48, H), BF16),
            vm((8, 2, 4, 48, H), BF16),
            vm((8, 4, 48, H), BF16),
            vm((8, 48, H), BF16),
            vm((8, 2, 48, H), BF16),
            vm((8, 2, 24, H), F32),
            vm((8, 24, H), F32),
            pltpu.SemaphoreType.DMA((25,)),
            pltpu.SemaphoreType.DMA((N_SEND,)),
            pltpu.SemaphoreType.DMA((N_SEND,)),
        ],
        compiler_params=pltpu.CompilerParams(
            collective_id=0, has_side_effects=True, vmem_limit_bytes=56 * 2**20
        ),
    )(
        tokens,
        jnp.transpose(attended, (1, 0, 2)),
        jnp.transpose(out_weight, (1, 0, 2)).reshape(E, 8 * E),
        cotangent,
    )
    return (
        mixed,
        jnp.transpose(gatt, (1, 0, 2)),
        jnp.transpose(wg, (1, 0, 2)),
    )


def solution(mesh):
    placed = (
        P("dp", "tensor"),
        P("dp", "tensor", None),
        P(None, "tensor", None),
        P("dp", "tensor"),
    )
    return jax.shard_map(
        body,
        mesh=mesh,
        in_specs=placed,
        out_specs=(P("dp", "tensor"), P("dp", "tensor", None), P("dp", "tensor", None)),
        check_vma=False,
    )
```

time: 319 us -> 75 us (0.24)
  waiting for transfers between devices: 259 us -> 0 us
  Pallas kernels: 0 us -> 72 us
  matrix products: 23.3 us -> 0 us
  local copies, waits for them, and re-layouts: 19.2 us -> 2.31 us
  between operations: 13.8 us -> 0.64 us
    reduce_scatter x2 -> x0, waiting for transfers between devices: 187 us -> none  [the longest x1 143 us: body(): lax.psum_scatter(term.astype(jnp.bfloat16), 'dp', scatter_dimension=0, ti...]
    pallas_call x0 -> x1, Pallas kernels: none -> 72 us  [body(): pl.pallas_call(functools.partial(kernel, factor), out_shape=(vm((T, E), B...]
    all_gather x1 -> x0, waiting for transfers between devices: 71.6 us -> none  [body(): whole_grad = lax.all_gather(cotangent, 'tensor', axis=1, tiled=True)]
    dot_general x3 -> x0, matrix products: 23.3 us -> none  [the longest x1 8.34 us: body(): jnp.einsum('the,td->ehd', attended, whole_grad, preferred_element_type=jn...]
    convert_element_type x1 -> x0, local copies, waits for them, and re-layouts: 16.1 us -> none  [body(): term.astype(jnp.bfloat16)]
  transfers between devices with their start and end apart: 3 -> 0, of which waited for: 3 -> 0; matrix products, arithmetic and copies ran while one was open for 13% -> 0% of each run, Pallas kernels for 0% -> 0%
where the time goes in v2:
time: 75 us; the launch traced here: 74.9 us
  Pallas kernels  72 us (96%)
  local copies, waits for them, and re-layouts  2.31 us (3%)
    pallas_call x1, Pallas kernels, body(): pl.pallas_call(functools.partial(kernel, factor), out_shape=(vm((T, E), B...  72 us
    unnamed x3, local copies, waits for them, and re-layouts  2.31 us

profile of v2, /device:TPU:1, one launch (start us, length us, event | category | flops | bytes accessed | tf_op | source)
XLA Modules:
  0.0 74.9 jit_solution(14559427250081973404)
XLA Ops:
  0.6 72.0 %shard_map.67 = (bf16[256,768]{1,0:T(8,128)(2,1)S(1)}, bf16[6,256,128]{2,1,0:T(8,128)(2,1)S(1)}, f32[6,4,6144]{2,1,0:T(4,128)S(1)}) custom-call(bf16[256,768]{1,0:T(8,128)(2,1)} %tok_hbm.1, bf16[6,256,128]{2,1,0:T(8,128)(2,1)} %bitcast.9, bf16[768,6144]{1,0:T(8,128)(2,1)} %bitcast.8, bf16[256,768]{1,0:T(8,128)(2,1)} %cot_hbm.1), custom_call_target="tpu_custom_call" | custom-call | tf_op jit(solution)/shard_map/pallas_call | solution.py:400
  72.6 0.7 copy.10
  73.4 0.7 copy.11
  74.1 0.8 %copy.12 = f32[4,6,6144]{2,0,1:T(4,128)} copy(f32[4,6,6144]{2,0,1:T(4,128)S(1)} %bitcast.6) | data formatting | bytes 1179648

commit v3 on v2

v3 whole, which is shorter than its diff:
```python
import functools
import math

import jax
import jax.numpy as jnp
from jax import lax
from jax.experimental import pallas as pl
from jax.experimental.pallas import tpu as pltpu
from jax.sharding import PartitionSpec as P

MESH = pl.DeviceIdType.MESH
F32 = jnp.float32
BF16 = jnp.bfloat16

Y_OFF = (0, 0, 3, 1, 3, 1, 2, 2)
Z_OFF = (0, 1, 0, 0, 1, 1, 0, 1)
T = 256
E = 768
H = 384
SPLIT = (7,)


def nt(a, b):
    return lax.dot_general(a, b, (((1,), (1,)), ((), ())), preferred_element_type=F32)


def nn(a, b):
    return lax.dot_general(a, b, (((1,), (0,)), ((), ())), preferred_element_type=F32)


def kernel(
    factor,
    tok_hbm, att_hbm, w_hbm, cot_hbm,
    mixed, gatt, wg,
    tok, a_own, perm, at, w, cot, part,
    bx, br, bfin, bz, gacc,
    term, xr, xfin, xs, zr, zfin, res, resx,
    lsem, ssem, rsem,
):
    dp, tp = lax.axis_index("dp"), lax.axis_index("tensor")
    x, zh, c = dp // 8, (dp // 2) % 4, dp % 2
    y, zl = tp // 2, tp % 2

    def dev(x_, zh_, c_, y_, zl_):
        return ((x_ * 4 + zh_) * 2 + c_, y_ * 2 + zl_)

    xp, xm = dev((x + 1) % 4, zh, c, y, zl), dev((x + 3) % 4, zh, c, y, zl)
    yp, ym = dev(x, zh, c, (y + 1) % 4, zl), dev(x, zh, c, (y + 3) % 4, zl)
    zp, zm = dev(x, (zh + 1) % 4, c, y, zl), dev(x, (zh + 3) % 4, c, y, zl)
    zo, co = dev(x, zh, c, y, 1 - zl), dev(x, zh, 1 - c, y, zl)

    barrier = pltpu.get_barrier_semaphore()
    for to in (xp, xm, yp, ym, zp, zm, zo, co):
        pl.semaphore_signal(barrier, inc=1, device_id=to, device_id_type=MESH)

    def slot(i, k):
        return (0, 2 + k, 3 - k, 1, 6, 4 + k, 5 - k, 7)[i]

    def block(s):
        return ((y + Y_OFF[s]) % 4) * 2 + (zl + Z_OFF[s]) % 2

    def step_block(i, k):
        yo = (0, 3 - 2 * k, 1 + 2 * k, 0, 2, 3 - 2 * k, 1 + 2 * k, 2)[i]
        return ((y + yo) % 4) * 2 + (zl + (0, 0, 0, 1, 0, 1, 1, 1)[i]) % 2

    count = [0]

    def load(src, dst):
        copy = pltpu.make_async_copy(src, dst, lsem.at[count[0]])
        count[0] += 1
        copy.start()
        return copy

    l_cot = [load(cot_hbm.at[:, pl.ds(H * h, H)], cot.at[0, 1 + h]) for h in range(2)]
    l_att = [load(att_hbm.at[h], a_own.at[:, pl.ds(128 * h, 128)]) for h in range(6)]
    sent = []

    def send(src, dst, to):
        i = len(sent)
        copy = pltpu.make_async_remote_copy(
            src_ref=src, dst_ref=dst, send_sem=ssem.at[i], recv_sem=rsem.at[i],
            device_id=to, device_id_type=MESH,
        )
        copy.start()
        sent.append(copy)
        return copy

    a, cx = {}, {}

    def a_send(src, s, h, to):
        a[s, h] = send(cot.at[src, 1 + h], cot.at[s, 1 + h], to)

    def core_send(i):
        s = slot(i, 1 - c)
        cx[i] = send(cot.at[s, 2 - c], cot.at[s, 3 * (1 - c)], co)

    def make_perm(i, _):
        row = lax.broadcasted_iota(jnp.int32, (48, 128), 0)
        core = (row >= 24).astype(jnp.int32)
        r = row - 24 * core
        want = (r >> 2) * 128 + 8 * i + 4 * core + (r & 3)
        want = want - lax.broadcasted_iota(jnp.int32, (48, 128), 1)
        rows = pl.ds(pl.multiple_of((i % 8) * 48, 16), 48)
        for h in range(6):
            perm[i // 8, rows, pl.ds(128 * h, 128)] = (
                jnp.where(want == 128 * h, 1.0, 0.0).astype(BF16)
            )
        return 0

    lax.fori_loop(0, 16, make_perm, 0)
    gacc[...] = jnp.zeros_like(gacc)
    pl.semaphore_wait(barrier, 8)
    l_cot[0].wait()
    l_cot[1].wait()
    a_send(0, 2, 0, yp)
    a_send(0, 3, 1, ym)
    a[1] = send(cot.at[0, pl.ds(1, 2)], cot.at[1, pl.ds(1, 2)], zo)
    core_send(0)
    a_send(0, 2, 1, yp)
    a_send(0, 3, 0, ym)
    l_w = {}
    for s in (7, 5, 4, 2, 3, 6, 1, 0):
        for h in range(2):
            col = pl.multiple_of(block(s) * E + H * h, 128)
            l_w[s, h] = load(w_hbm.at[:, pl.ds(col, H)], w.at[s, h])
    l_tok = load(tok_hbm, tok)

    for cp in l_att:
        cp.wait()
    mine = pl.ds(pl.multiple_of(T * (1 - c), T), T)

    def permute(i, _):
        at[i, :, mine] = nt(perm[i], a_own[...]).astype(BF16)
        return 0

    lax.fori_loop(0, 2, permute, 0)
    a_swap = send(at.at[:, :, mine], at.at[:, :, mine], co)

    x1, x2, zf, zn, zt, r1 = {}, {}, {}, {}, {}, {}
    xf, xn, xl = (x + 2) % 4, (x + 1) % 4, (x + 3) % 4

    def c_term(i):
        cx[i].wait_recv()
        s = slot(i, c)

        val = nn(at[...].reshape(E, 2 * T), cot[s, pl.ds(2 * c, 2)].reshape(2 * T, H))
        term[i] = val.astype(BF16).reshape(4, 4, 48, H)
        for u in range(2 if i in SPLIT else 1):
            p, q = x_parts(i, u)
            x1[i, u] = [
                send(term.at[i, xf, p], xr.at[i, 0, p], xp),
                send(term.at[i, xf, q], xr.at[i, 1, q], xm),
                send(term.at[i, xn, q], xfin.at[i, 0, q], xp),
                send(term.at[i, xl, p], xfin.at[i, 1, p], xm),
            ]

    def x_parts(i, u):
        if i not in SPLIT:
            return pl.ds(0, 2), pl.ds(2, 2)
        n_p, n_m, _, _ = z_places(i)
        p, q = (((zh + 2) % 4, n_p), (n_m, zh))[u]
        return pl.ds(p, 1), pl.ds(q, 1)

    def c_relay(i, u=0):
        p, q = x_parts(i, u)
        x1[i, u][0].wait_recv()
        t = term[i, xn, p].astype(F32) + xr[i, 0, p].astype(F32)
        term[i, xn, p] = t.astype(BF16)
        x2[i, u] = [send(term.at[i, xn, p], xfin.at[i, 0, p], xp)]
        x1[i, u][1].wait_recv()
        t = term[i, xl, q].astype(F32) + xr[i, 1, q].astype(F32)
        term[i, xl, q] = t.astype(BF16)
        x2[i, u].append(send(term.at[i, xl, q], xfin.at[i, 1, q], xm))

    def z_places(i):
        up, down = (zh + 1) % 4, (zh + 3) % 4
        return (up, down, zp, zm) if i % 2 == 0 else (down, up, zm, zp)

    def c_xsum(i, u=0):
        for cp in x1[i, u][2:] + x2[i, u]:
            cp.wait_recv()
        _, n_m, to_p, to_m = z_places(i)
        for part_z in x_parts(i, u) if i in SPLIT else (pl.ds(0, 4),):
            t = term[i, x, part_z].astype(F32) + xfin[i, 0, part_z].astype(F32)
            xs[i, part_z] = (t + xfin[i, 1, part_z].astype(F32)).astype(BF16)
        if u == 0:
            zf[i] = send(xs.at[i, (zh + 2) % 4], zr.at[i], to_p)
        if u == 1 or i not in SPLIT:
            zn[i] = send(xs.at[i, n_m], zfin.at[i, 1], to_m)

    def c_zrelay(i):
        n_p, _, to_p, _ = z_places(i)
        zf[i].wait_recv()
        t = xs[i, n_p].astype(F32) + zr[i].astype(F32)
        xs[i, n_p] = t.astype(BF16)
        zt[i] = send(xs.at[i, n_p], zfin.at[i, 0], to_p)

    def put(val, col):
        cols = pl.ds(pl.multiple_of(col, 128), H)
        for h in range(6):
            wg[h, :, cols] = val[4 * h : 4 * h + 4]

    def c_zsum(i):
        zn[i].wait_recv()
        zt[i].wait_recv()
        t = xs[i, zh].astype(F32) + zfin[i, 0].astype(F32) + zfin[i, 1].astype(F32)
        res[i] = (t * factor).reshape(2, 24, H)
        r1[i] = send(res.at[i, 1 - c], resx.at[i], co)
        put(res[i, c], step_block(i, c) * E + H * c)

    def c_out(i):
        r1[i].wait_recv()
        put(resx[i], step_block(i, 1 - c) * E + H * (1 - c))

    def grad(s):
        def go(b, _):
            cols = pl.ds(pl.multiple_of(b * T, T), T)
            t = nt(cot[s, 1], w[s, 0, cols]) + nt(cot[s, 2], w[s, 1, cols])
            gacc[:, cols] += t
            return 0

        lax.fori_loop(0, 3, go, 0)

    def b_part(s):
        for h in range(2):
            l_w[s, h].wait()

        def go(h, _):
            part[s, h] = nn(a_own[...], w[s, h]).astype(BF16)
            return 0

        lax.fori_loop(0, 2, go, 0)

    b1 = {}

    def b_over():
        b1["x"] = send(part.at[7], bx, zo)

    def b_near(r):
        if r == 0:
            b1["n0"] = [
                send(part.at[5], bfin.at[0, 0], yp),
                send(part.at[4], bfin.at[0, 1], ym),
            ]
        else:
            b1["n1"] = [
                send(part.at[3, 1], bfin.at[1, 0, 1], yp),
                send(part.at[2, 0], bfin.at[1, 1, 0], ym),
            ]

    def add_to(s, h, ref):
        part[s, h] = (part[s, h].astype(F32) + ref[h].astype(F32)).astype(BF16)

    def b_far():
        b1["f"] = []
        b1["x"].wait_recv()
        for h, to in ((0, yp), (1, ym)):
            add_to(6, h, bx)
            b1["f"].append(send(part.at[6, h], br.at[h], to))

    def b_relay():
        b1["r"] = []
        for h, s, to in ((0, 3, yp), (1, 2, ym)):
            b1["f"][h].wait_recv()
            add_to(s, h, br)
            b1["r"].append(send(part.at[s, h], bfin.at[1, h, h], to))

    def b_sum(r, h):
        t = part[1 - r, h].astype(F32) + bfin[r, 0, h].astype(F32)
        return t + bfin[r, 1, h].astype(F32)

    def b_cross():
        for cp in b1["n0"]:
            cp.wait_recv()
        for h in range(2):
            part[1, h] = b_sum(0, h).astype(BF16)
        b1["c"] = send(part.at[1], bz, zo)

    def b_mix():
        for cp in b1["n1"] + b1["r"]:
            cp.wait_recv()
        l_tok.wait()
        b1["c"].wait_recv()
        for h in range(2):
            t = b_sum(1, h) + bz[h].astype(F32)
            cols = pl.ds(H * h, H)
            mixed[:, cols] = (tok[:, cols].astype(F32) + t).astype(BF16)

    def grad_out():
        for h in range(6):
            gatt[h] = gacc[:, pl.ds(128 * h, 128)].astype(BF16)

    drained = [0]

    def drain(n):
        for cp in sent[drained[0] : n]:
            cp.wait_send()
        drained[0] = max(drained[0], n)

    def arrived(*keys):
        for k in keys:
            a[k].wait_recv()

    b_part(7)
    a_swap.wait_recv()
    c_term(0)
    b_part(3)
    b_part(5)
    b_part(4)
    arrived((2, 0), (3, 1))
    a_send(2, 6, 0, yp)
    a_send(3, 6, 1, ym)
    core_send(1)
    c_relay(0)
    b_part(6)
    c_term(1)
    arrived((2, 1), (3, 0))
    core_send(2)
    b_over()
    arrived(1)
    a_send(1, 4, 1, yp)
    a_send(1, 5, 0, ym)
    c_term(2)
    c_relay(1)
    c_xsum(0)
    core_send(3)
    a_send(1, 4, 0, yp)
    a_send(1, 5, 1, ym)
    b_part(2)
    arrived((6, 0), (6, 1))
    core_send(4)
    c_term(3)
    c_relay(2)
    b_near(0)
    b_part(1)
    drain(11)
    arrived((4, 1), (5, 0))
    core_send(6)
    c_xsum(1)
    c_relay(3)
    c_term(6)
    arrived((4, 0), (5, 1))
    a_send(4, 7, 0, yp)
    a_send(5, 7, 1, ym)
    core_send(5)
    grad(1)
    drain(23)
    c_zrelay(0)
    c_xsum(2)
    b_near(1)
    c_term(4)
    c_xsum(3)
    drain(34)
    c_term(5)
    c_relay(6)
    grad(2)
    drain(40)
    c_zrelay(1)
    b_far()
    c_zrelay(2)
    c_zrelay(3)
    c_relay(4)
    b_cross()
    grad(6)
    drain(48)
    arrived((7, 0), (7, 1))
    core_send(7)
    c_relay(5)
    c_term(7)
    grad(4)
    drain(59)
    grad(3)
    c_zsum(3)
    c_xsum(4)
    c_relay(7, 0)
    c_xsum(5)
    drain(66)
    b_part(0)
    c_relay(7, 1)
    grad(7)
    c_xsum(7, 0)
    c_xsum(6)
    b_relay()
    grad(5)
    drain(73)
    c_zrelay(4)
    c_zsum(2)
    c_zrelay(5)
    c_xsum(7, 1)
    c_zsum(0)
    c_zrelay(7)
    c_zrelay(6)
    c_zsum(1)
    drain(81)
    grad(0)
    c_out(1)
    c_out(0)
    grad_out()
    b_mix()
    c_zsum(5)
    c_out(2)
    c_zsum(7)
    c_zsum(4)
    c_zsum(6)
    c_out(7)
    c_out(5)
    c_out(3)
    c_out(4)
    c_out(6)
    drain(len(sent))


N_SEND = 130


def body(tokens, attended, out_weight, cotangent):
    factor = 1.0 / math.sqrt(attended.shape[0] * lax.axis_size("dp"))
    any_spec = pl.BlockSpec(memory_space=pl.ANY)
    vm = pltpu.VMEM
    mixed, gatt, wg = pl.pallas_call(
        functools.partial(kernel, factor),
        out_shape=(
            vm((T, E), BF16),
            vm((6, T, 128), BF16),
            vm((6, 4, 8 * E), F32),
        ),
        in_specs=[any_spec] * 4,
        out_specs=(pl.BlockSpec(memory_space=vm),) * 3,
        scratch_shapes=[
            vm((T, E), BF16),
            vm((T, E), BF16),
            vm((2, H, E), BF16),
            vm((2, H, 2 * T), BF16),
            vm((8, 2, E, H), BF16),
            vm((8, 4, T, H), BF16),
            vm((8, 2, T, H), BF16),
            vm((2, T, H), BF16),
            vm((2, T, H), BF16),
            vm((2, 2, 2, T, H), BF16),
            vm((2, T, H), BF16),
            vm((T, E), F32),
            vm((8, 4, 4, 48, H), BF16),
            vm((8, 2, 4, 48, H), BF16),
            vm((8, 2, 4, 48, H), BF16),
            vm((8, 4, 48, H), BF16),
            vm((8, 48, H), BF16),
            vm((8, 2, 48, H), BF16),
            vm((8, 2, 24, H), F32),
            vm((8, 24, H), F32),
            pltpu.SemaphoreType.DMA((25,)),
            pltpu.SemaphoreType.DMA((N_SEND,)),
            pltpu.SemaphoreType.DMA((N_SEND,)),
        ],
        compiler_params=pltpu.CompilerParams(
            collective_id=0, has_side_effects=True, vmem_limit_bytes=56 * 2**20
        ),
    )(
        tokens,
        jnp.transpose(attended, (1, 0, 2)),
        jnp.transpose(out_weight, (1, 0, 2)).reshape(E, 8 * E),
        cotangent,
    )
    return (
        mixed,
        jnp.transpose(gatt, (1, 0, 2)),
        jnp.transpose(wg, (1, 0, 2)),
    )


def solution(mesh):
    placed = (
        P("dp", "tensor"),
        P("dp", "tensor", None),
        P(None, "tensor", None),
        P("dp", "tensor"),
    )
    return jax.shard_map(
        body,
        mesh=mesh,
        in_specs=placed,
        out_specs=(P("dp", "tensor"), P("dp", "tensor", None), P("dp", "tensor", None)),
        check_vma=False,
    )
```

time: 75 us -> 70.8 us (0.944)
  Pallas kernels: 72 us -> 67.7 us
    pallas_call x1, Pallas kernels: 72 us -> 67.7 us  [body(): pl.pallas_call(functools.partial(kernel, factor), out_shape=(vm((T, E), B...]
where the time goes in v3:
time: 70.8 us; the launch traced here: 70.7 us
  Pallas kernels  67.7 us (96%)
  local copies, waits for them, and re-layouts  2.31 us (3%)
    pallas_call x1, Pallas kernels, body(): pl.pallas_call(functools.partial(kernel, factor), out_shape=(vm((T, E), B...  67.7 us
    unnamed x3, local copies, waits for them, and re-layouts  2.31 us

profile of v3, /device:TPU:1, one launch (start us, length us, event | category | flops | bytes accessed | tf_op | source)
XLA Modules:
  0.0 70.7 jit_solution(11273873405231544626)
XLA Ops:
  0.6 67.7 %shard_map.67 = (bf16[256,768]{1,0:T(8,128)(2,1)S(1)}, bf16[6,256,128]{2,1,0:T(8,128)(2,1)S(1)}, f32[6,4,6144]{2,1,0:T(4,128)S(1)}) custom-call(bf16[256,768]{1,0:T(8,128)(2,1)} %tok_hbm.1, bf16[6,256,128]{2,1,0:T(8,128)(2,1)} %bitcast.9, bf16[768,6144]{1,0:T(8,128)(2,1)} %bitcast.8, bf16[256,768]{1,0:T(8,128)(2,1)} %cot_hbm.1), custom_call_target="tpu_custom_call" | custom-call | tf_op jit(solution)/shard_map/pallas_call | solution.py:420
  68.4 0.7 %copy.10 = bf16[256,768]{1,0:T(8,128)(2,1)} copy(bf16[256,768]{1,0:T(8,128)(2,1)S(1)} %get-tuple-element.9) | data formatting | bytes 786432
  69.1 0.7 %copy.11 = bf16[256,6,128]{2,0,1:T(8,128)(2,1)} copy(bf16[256,6,128]{2,0,1:T(8,128)(2,1)S(1)} %bitcast.7) | data formatting | bytes 786432
  69.9 0.8 %copy.12 = f32[4,6,6144]{2,0,1:T(4,128)} copy(f32[4,6,6144]{2,0,1:T(4,128)S(1)} %bitcast.6) | data formatting | bytes 1179648

commit v4 on v3

--- a/solution.py
+++ b/solution.py
@@ -145,11 +145,14 @@
 
         val = nn(at[...].reshape(E, 2 * T), cot[s, pl.ds(2 * c, 2)].reshape(2 * T, H))
         term[i] = val.astype(BF16).reshape(4, 4, 48, H)
-        for u in range(2 if i in SPLIT else 1):
-            p, q = x_parts(i, u)
+        parts = [x_parts(i, u) for u in range(2 if i in SPLIT else 1)]
+        for u, (p, q) in enumerate(parts):
             x1[i, u] = [
                 send(term.at[i, xf, p], xr.at[i, 0, p], xp),
                 send(term.at[i, xf, q], xr.at[i, 1, q], xm),
+            ]
+        for u, (p, q) in enumerate(parts):
+            x1[i, u] += [
                 send(term.at[i, xn, q], xfin.at[i, 0, q], xp),
                 send(term.at[i, xl, p], xfin.at[i, 1, p], xm),
             ]
@@ -233,28 +236,28 @@
 
     b1 = {}
 
-    def b_over():
-        b1["x"] = send(part.at[7], bx, zo)
-
-    def b_near(r):
-        if r == 0:
-            b1["n0"] = [
-                send(part.at[5], bfin.at[0, 0], yp),
-                send(part.at[4], bfin.at[0, 1], ym),
-            ]
-        else:
-            b1["n1"] = [
-                send(part.at[3, 1], bfin.at[1, 0, 1], yp),
-                send(part.at[2, 0], bfin.at[1, 1, 0], ym),
-            ]
+    def b_over(h):
+        b1["x", h] = send(part.at[7, h], bx.at[h], zo)
+
+    def b_near(h):
+        b1["n", h] = [
+            send(part.at[5, h], bfin.at[0, 0, h], yp),
+            send(part.at[4, h], bfin.at[0, 1, h], ym),
+        ]
+
+    def b_beside():
+        b1["b"] = [
+            send(part.at[3, 1], bfin.at[1, 0, 1], yp),
+            send(part.at[2, 0], bfin.at[1, 1, 0], ym),
+        ]
 
     def add_to(s, h, ref):
         part[s, h] = (part[s, h].astype(F32) + ref[h].astype(F32)).astype(BF16)
 
     def b_far():
         b1["f"] = []
-        b1["x"].wait_recv()
         for h, to in ((0, yp), (1, ym)):
+            b1["x", h].wait_recv()
             add_to(6, h, bx)
             b1["f"].append(send(part.at[6, h], br.at[h], to))
 
@@ -265,23 +268,24 @@
             add_to(s, h, br)
             b1["r"].append(send(part.at[s, h], bfin.at[1, h, h], to))
 
-    def b_sum(r, h):
-        t = part[1 - r, h].astype(F32) + bfin[r, 0, h].astype(F32)
-        return t + bfin[r, 1, h].astype(F32)
-
-    def b_cross():
-        for cp in b1["n0"]:
+    def b_sum(r, h, rows=slice(None)):
+        t = part[1 - r, h, rows].astype(F32) + bfin[r, 0, h, rows].astype(F32)
+        return t + bfin[r, 1, h, rows].astype(F32)
+
+    def b_cross(h, k):
+        for cp in b1.pop(("n", h), ()):
             cp.wait_recv()
-        for h in range(2):
-            part[1, h] = b_sum(0, h).astype(BF16)
-        b1["c"] = send(part.at[1], bz, zo)
+        rows = pl.ds(k * (T // 2), T // 2)
+        part[1, h, rows] = b_sum(0, h, rows).astype(BF16)
+        b1["c", h, k] = send(part.at[1, h, rows], bz.at[h, rows], zo)
 
     def b_mix():
-        for cp in b1["n1"] + b1["r"]:
+        for cp in b1["b"] + b1["r"]:
             cp.wait_recv()
         l_tok.wait()
-        b1["c"].wait_recv()
         for h in range(2):
+            b1["c", h, 0].wait_recv()
+            b1["c", h, 1].wait_recv()
             t = b_sum(1, h) + bz[h].astype(F32)
             cols = pl.ds(H * h, H)
             mixed[:, cols] = (tok[:, cols].astype(F32) + t).astype(BF16)
@@ -302,111 +306,117 @@
             a[k].wait_recv()
 
     b_part(7)
+    b_part(3)
     a_swap.wait_recv()
     c_term(0)
-    b_part(3)
+    b_part(4)
     b_part(5)
-    b_part(4)
+    b_over(1)
+    b_near(0)
     arrived((2, 0), (3, 1))
     a_send(2, 6, 0, yp)
     a_send(3, 6, 1, ym)
     core_send(1)
+    b_part(2)
     c_relay(0)
-    b_part(6)
     c_term(1)
+    b_part(1)
+    arrived(1)
+    core_send(3)
     arrived((2, 1), (3, 0))
     core_send(2)
-    b_over()
-    arrived(1)
+    grad(1)
+    c_term(3)
+    c_xsum(0)
+    a_send(1, 4, 0, yp)
+    a_send(1, 5, 1, ym)
+    c_term(2)
+    grad(2)
+    b_cross(0, 1)
     a_send(1, 4, 1, yp)
     a_send(1, 5, 0, ym)
-    c_term(2)
+    b_part(6)
+    drain(7)
+    b_cross(0, 0)
+    c_zrelay(0)
+    c_relay(3)
+    b_over(0)
+    b_near(1)
     c_relay(1)
-    c_xsum(0)
-    core_send(3)
-    a_send(1, 4, 0, yp)
-    a_send(1, 5, 1, ym)
-    b_part(2)
     arrived((6, 0), (6, 1))
     core_send(4)
-    c_term(3)
+    grad(3)
+    drain(17)
     c_relay(2)
-    b_near(0)
-    b_part(1)
-    drain(11)
-    arrived((4, 1), (5, 0))
-    core_send(6)
-    c_xsum(1)
-    c_relay(3)
-    c_term(6)
+    c_term(4)
     arrived((4, 0), (5, 1))
     a_send(4, 7, 0, yp)
     a_send(5, 7, 1, ym)
     core_send(5)
-    grad(1)
-    drain(23)
-    c_zrelay(0)
+    c_xsum(3)
+    drain(28)
+    c_xsum(1)
+    c_term(5)
     c_xsum(2)
-    b_near(1)
-    c_term(4)
-    c_xsum(3)
-    drain(34)
-    c_term(5)
-    c_relay(6)
-    grad(2)
-    drain(40)
-    c_zrelay(1)
+    drain(36)
+    b_part(0)
+    arrived((4, 1), (5, 0))
+    core_send(6)
+    grad(0)
+    c_relay(4)
+    c_term(6)
+    c_zrelay(3)
+    b_cross(1, 1)
+    c_zsum(0)
+    drain(46)
     b_far()
-    c_zrelay(2)
-    c_zrelay(3)
-    c_relay(4)
-    b_cross()
+    c_relay(5)
     grad(6)
-    drain(48)
+    b_beside()
+    c_xsum(4)
+    drain(54)
     arrived((7, 0), (7, 1))
     core_send(7)
-    c_relay(5)
+    b_cross(1, 0)
+    c_relay(6)
+    c_zrelay(2)
     c_term(7)
+    c_zrelay(1)
+    c_xsum(5)
+    drain(70)
     grad(4)
-    drain(59)
-    grad(3)
+    c_relay(7, 0)
+    c_xsum(6)
+    c_relay(7, 1)
+    b_relay()
+    c_out(0)
+    drain(78)
+    grad(5)
+    c_zrelay(4)
+    c_xsum(7, 0)
+    c_zsum(2)
+    c_zrelay(6)
+    c_zrelay(5)
     c_zsum(3)
-    c_xsum(4)
-    c_relay(7, 0)
-    c_xsum(5)
-    drain(66)
-    b_part(0)
-    c_relay(7, 1)
+    drain(84)
     grad(7)
-    c_xsum(7, 0)
-    c_xsum(6)
-    b_relay()
-    grad(5)
-    drain(73)
-    c_zrelay(4)
-    c_zsum(2)
-    c_zrelay(5)
     c_xsum(7, 1)
-    c_zsum(0)
     c_zrelay(7)
-    c_zrelay(6)
+    c_zsum(6)
+    c_out(3)
+    c_zsum(4)
     c_zsum(1)
-    drain(81)
-    grad(0)
+    grad_out()
+    c_zsum(5)
+    drain(90)
+    b_mix()
+    c_zsum(7)
     c_out(1)
-    c_out(0)
-    grad_out()
-    b_mix()
-    c_zsum(5)
+    c_out(6)
     c_out(2)
-    c_zsum(7)
-    c_zsum(4)
-    c_zsum(6)
+    c_out(5)
+    c_out(4)
     c_out(7)
-    c_out(5)
-    c_out(3)
-    c_out(4)
-    c_out(6)
     drain(len(sent))
 
 

time: 70.8 us -> 68.6 us (0.969)
  Pallas kernels: 67.7 us -> 65.6 us
    pallas_call x1, Pallas kernels: 67.7 us -> 65.6 us  [body(): pl.pallas_call(functools.partial(kernel, factor), out_shape=(vm((T, E), B...]
where the time goes in v4:
time: 68.6 us; the launch traced here: 68.5 us
  Pallas kernels  65.6 us (96%)
  local copies, waits for them, and re-layouts  2.31 us (3%)
    pallas_call x1, Pallas kernels, body(): pl.pallas_call(functools.partial(kernel, factor), out_shape=(vm((T, E), B...  65.6 us
    unnamed x3, local copies, waits for them, and re-layouts  2.31 us

profile of v4, /device:TPU:1, one launch (start us, length us, event | category | flops | bytes accessed | tf_op | source)
XLA Modules:
  0.0 68.5 jit_solution(13576144420256771504)
XLA Ops:
  0.6 65.6 %shard_map.67 = (bf16[256,768]{1,0:T(8,128)(2,1)S(1)}, bf16[6,256,128]{2,1,0:T(8,128)(2,1)S(1)}, f32[6,4,6144]{2,1,0:T(4,128)S(1)}) custom-call(bf16[256,768]{1,0:T(8,128)(2,1)} %tok_hbm.1, bf16[6,256,128]{2,1,0:T(8,128)(2,1)} %bitcast.9, bf16[768,6144]{1,0:T(8,128)(2,1)} %bitcast.8, bf16[256,768]{1,0:T(8,128)(2,1)} %cot_hbm.1), custom_call_target="tpu_custom_call" | custom-call | tf_op jit(solution)/shard_map/pallas_call | solution.py:430
  66.2 0.7 %copy.10 = bf16[256,768]{1,0:T(8,128)(2,1)} copy(bf16[256,768]{1,0:T(8,128)(2,1)S(1)} %get-tuple-element.9) | data formatting | bytes 786432
  67.0 0.7 %copy.11 = bf16[256,6,128]{2,0,1:T(8,128)(2,1)} copy(bf16[256,6,128]{2,0,1:T(8,128)(2,1)S(1)} %bitcast.7) | data formatting | bytes 786432
  67.7 0.8 %copy.12 = f32[4,6,6144]{2,0,1:T(4,128)} copy(f32[4,6,6144]{2,0,1:T(4,128)S(1)} %bitcast.6) | data formatting | bytes 1179648

commit v5 on v4

--- a/solution.py
+++ b/solution.py
@@ -17,7 +17,7 @@
 T = 256
 E = 768
 H = 384
-SPLIT = (7,)
+SPLIT = (6, 7, )
 
 
 def nt(a, b):
@@ -114,7 +114,7 @@
     l_cot[1].wait()
     a_send(0, 2, 0, yp)
     a_send(0, 3, 1, ym)
-    a[1] = send(cot.at[0, pl.ds(1, 2)], cot.at[1, pl.ds(1, 2)], zo)
+    a[1] = [send(cot.at[0, pl.ds(1, 2)], cot.at[1, pl.ds(1, 2)], zo)]
     core_send(0)
     a_send(0, 2, 1, yp)
     a_send(0, 3, 0, ym)
@@ -129,12 +129,10 @@
         cp.wait()
     mine = pl.ds(pl.multiple_of(T * (1 - c), T), T)
 
-    def permute(i, _):
+    a_swap = []
+    for i in range(2):
         at[i, :, mine] = nt(perm[i], a_own[...]).astype(BF16)
-        return 0
-
-    lax.fori_loop(0, 2, permute, 0)
-    a_swap = send(at.at[:, :, mine], at.at[:, :, mine], co)
+        a_swap.append(send(at.at[i, :, mine], at.at[i, :, mine], co))
 
     x1, x2, zf, zn, zt, r1 = {}, {}, {}, {}, {}, {}
     xf, xn, xl = (x + 2) % 4, (x + 1) % 4, (x + 3) % 4
@@ -151,11 +149,13 @@
                 send(term.at[i, xf, p], xr.at[i, 0, p], xp),
                 send(term.at[i, xf, q], xr.at[i, 1, q], xm),
             ]
-        for u, (p, q) in enumerate(parts):
-            x1[i, u] += [
-                send(term.at[i, xn, q], xfin.at[i, 0, q], xp),
-                send(term.at[i, xl, p], xfin.at[i, 1, p], xm),
-            ]
+
+    def c_near(i, u=0):
+        p, q = x_parts(i, u)
+        x1[i, u] += [
+            send(term.at[i, xn, q], xfin.at[i, 0, q], xp),
+            send(term.at[i, xl, p], xfin.at[i, 1, p], xm),
+        ]
 
     def x_parts(i, u):
         if i not in SPLIT:
@@ -176,8 +176,9 @@
         x2[i, u].append(send(term.at[i, xl, q], xfin.at[i, 1, q], xm))
 
     def z_places(i):
-        up, down = (zh + 1) % 4, (zh + 3) % 4
-        return (up, down, zp, zm) if i % 2 == 0 else (down, up, zm, zp)
+        way = 1 + 2 * ((i + zl + 1) % 2)
+        n_p, n_m = (zh + way) % 4, (zh + 4 - way) % 4
+        return n_p, n_m, dev(x, n_p, c, y, zl), dev(x, n_m, c, y, zl)
 
     def c_xsum(i, u=0):
         for cp in x1[i, u][2:] + x2[i, u]:
@@ -215,7 +216,14 @@
         r1[i].wait_recv()
         put(resx[i], step_block(i, 1 - c) * E + H * (1 - c))
 
+    def w_ready(s):
+        for h in range(2):
+            if (s, h) in l_w:
+                l_w.pop((s, h)).wait()
+
     def grad(s):
+        w_ready(s)
+
         def go(b, _):
             cols = pl.ds(pl.multiple_of(b * T, T), T)
             t = nt(cot[s, 1], w[s, 0, cols]) + nt(cot[s, 2], w[s, 1, cols])
@@ -225,8 +233,7 @@
         lax.fori_loop(0, 3, go, 0)
 
     def b_part(s):
-        for h in range(2):
-            l_w[s, h].wait()
+        w_ready(s)
 
         def go(h, _):
             part[s, h] = nn(a_own[...], w[s, h]).astype(BF16)
@@ -303,124 +310,139 @@
 
     def arrived(*keys):
         for k in keys:
-            a[k].wait_recv()
+            for cp in a[k] if k == 1 else [a[k]]:
+                cp.wait_recv()
 
     b_part(7)
-    b_part(3)
-    a_swap.wait_recv()
+    for cp in a_swap:
+        cp.wait_recv()
     c_term(0)
+    c_near(0)
     b_part(4)
     b_part(5)
-    b_over(1)
-    b_near(0)
+    grad(0)
     arrived((2, 0), (3, 1))
     a_send(2, 6, 0, yp)
     a_send(3, 6, 1, ym)
     core_send(1)
-    b_part(2)
     c_relay(0)
     c_term(1)
-    b_part(1)
+    c_near(1)
     arrived(1)
     core_send(3)
+    b_part(1)
+    a_send(1, 4, 0, yp)
+    a_send(1, 5, 1, ym)
+    b_over(0)
+    c_term(3)
+    c_near(3)
+    c_xsum(0)
+    c_relay(1)
+    b_part(6)
+    b_near(0)
+    arrived((6, 0), (6, 1))
+    core_send(4)
+    b_over(1)
+    a_send(1, 4, 1, yp)
+    a_send(1, 5, 0, ym)
     arrived((2, 1), (3, 0))
     core_send(2)
-    grad(1)
-    c_term(3)
-    c_xsum(0)
-    a_send(1, 4, 0, yp)
-    a_send(1, 5, 1, ym)
-    c_term(2)
-    grad(2)
-    b_cross(0, 1)
-    a_send(1, 4, 1, yp)
-    a_send(1, 5, 0, ym)
-    b_part(6)
+    grad(3)
     drain(7)
-    b_cross(0, 0)
-    c_zrelay(0)
     c_relay(3)
-    b_over(0)
-    b_near(1)
-    c_relay(1)
-    arrived((6, 0), (6, 1))
-    core_send(4)
-    grad(3)
-    drain(17)
-    c_relay(2)
     c_term(4)
     arrived((4, 0), (5, 1))
     a_send(4, 7, 0, yp)
     a_send(5, 7, 1, ym)
     core_send(5)
-    c_xsum(3)
-    drain(28)
+    b_part(3)
+    drain(14)
+    c_near(4)
     c_xsum(1)
     c_term(5)
-    c_xsum(2)
-    drain(36)
-    b_part(0)
+    b_part(2)
+    drain(20)
+    c_xsum(3)
+    b_cross(0, 1)
+    c_relay(4)
+    c_term(2)
+    b_cross(0, 0)
+    grad(1)
+    drain(28)
+    c_near(5)
+    b_near(1)
+    c_relay(5)
+    c_zrelay(1)
+    c_near(2)
     arrived((4, 1), (5, 0))
     core_send(6)
-    grad(0)
-    c_relay(4)
+    c_xsum(4)
+    drain(40)
+    b_part(0)
+    c_zrelay(0)
     c_term(6)
+    c_relay(2)
     c_zrelay(3)
-    b_cross(1, 1)
-    c_zsum(0)
-    drain(46)
-    b_far()
-    c_relay(5)
-    grad(6)
-    b_beside()
-    c_xsum(4)
-    drain(54)
     arrived((7, 0), (7, 1))
     core_send(7)
+    c_zrelay(4)
+    c_near(6, 0)
+    b_far()
+    c_xsum(5)
+    drain(56)
+    c_term(7)
+    c_relay(6, 0)
+    b_cross(1, 1)
     b_cross(1, 0)
-    c_relay(6)
-    c_zrelay(2)
-    c_term(7)
-    c_zrelay(1)
-    c_xsum(5)
-    drain(70)
+    c_near(7, 0)
     grad(4)
+    drain(66)
+    c_relay(6, 1)
+    c_xsum(2)
+    c_zsum(4)
     c_relay(7, 0)
-    c_xsum(6)
-    c_relay(7, 1)
-    b_relay()
-    c_out(0)
-    drain(78)
-    grad(5)
-    c_zrelay(4)
-    c_xsum(7, 0)
-    c_zsum(2)
-    c_zrelay(6)
+    b_beside()
     c_zrelay(5)
     c_zsum(3)
+    drain(77)
+    c_near(6, 1)
+    c_relay(7, 1)
+    c_xsum(6, 0)
+    c_near(7, 1)
+    grad(6)
     drain(84)
-    grad(7)
+    c_zsum(1)
+    c_xsum(7, 0)
+    b_relay()
+    c_out(3)
+    c_xsum(6, 1)
+    c_zrelay(2)
+    c_zsum(0)
+    drain(91)
+    grad(2)
+    c_zrelay(6)
+    c_zsum(5)
     c_xsum(7, 1)
     c_zrelay(7)
+    grad(5)
+    c_out(0)
+    c_out(4)
+    c_zsum(2)
+    grad(7)
+    c_out(2)
+    grad_out()
+    c_out(1)
     c_zsum(6)
-    c_out(3)
-    c_zsum(4)
-    c_zsum(1)
-    grad_out()
-    c_zsum(5)
-    drain(90)
+    drain(97)
+    c_out(5)
+    c_zsum(7)
     b_mix()
-    c_zsum(7)
-    c_out(1)
     c_out(6)
-    c_out(2)
-    c_out(5)
-    c_out(4)
     c_out(7)
     drain(len(sent))
 
 
-N_SEND = 130
+N_SEND = 144
 
 
 def body(tokens, attended, out_weight, cotangent):

time: 68.6 us -> 68.3 us (level)
  no operation moved by 1% of the time
where the time goes in v5:
time: 68.3 us; the launch traced here: 68.2 us
  Pallas kernels  65.3 us (96%)
  local copies, waits for them, and re-layouts  2.31 us (3%)
    pallas_call x1, Pallas kernels, body(): pl.pallas_call(functools.partial(kernel, factor), out_shape=(vm((T, E), B...  65.3 us
    unnamed x3, local copies, waits for them, and re-layouts  2.31 us

profile of v5, /device:TPU:1, one launch (start us, length us, event | category | flops | bytes accessed | tf_op | source)
XLA Modules:
  0.0 68.2 jit_solution(7248749852825733986)
XLA Ops:
  0.6 65.3 %shard_map.67 = (bf16[256,768]{1,0:T(8,128)(2,1)S(1)}, bf16[6,256,128]{2,1,0:T(8,128)(2,1)S(1)}, f32[6,4,6144]{2,1,0:T(4,128)S(1)}) custom-call(bf16[256,768]{1,0:T(8,128)(2,1)} %tok_hbm.1, bf16[6,256,128]{2,1,0:T(8,128)(2,1)} %bitcast.9, bf16[768,6144]{1,0:T(8,128)(2,1)} %bitcast.8, bf16[256,768]{1,0:T(8,128)(2,1)} %cot_hbm.1), custom_call_target="tpu_custom_call" | custom-call | tf_op jit(solution)/shard_map/pallas_call | solution.py:452
  65.9 0.7 %copy.10 = bf16[256,768]{1,0:T(8,128)(2,1)} copy(bf16[256,768]{1,0:T(8,128)(2,1)S(1)} %get-tuple-element.9) | data formatting | bytes 786432
  66.7 0.7 %copy.11 = bf16[256,6,128]{2,0,1:T(8,128)(2,1)} copy(bf16[256,6,128]{2,0,1:T(8,128)(2,1)S(1)} %bitcast.7) | data formatting | bytes 786432
  67.4 0.8 %copy.12 = f32[4,6,6144]{2,0,1:T(4,128)} copy(f32[4,6,6144]{2,0,1:T(4,128)S(1)} %bitcast.6) | data formatting | bytes 1179648

commit v6 on v5

--- a/solution.py
+++ b/solution.py
@@ -119,12 +119,13 @@
     a_send(0, 2, 1, yp)
     a_send(0, 3, 0, ym)
     l_w = {}
-    for s in (7, 5, 4, 2, 3, 6, 1, 0):
+
+    def load_w(s):
         for h in range(2):
             col = pl.multiple_of(block(s) * E + H * h, 128)
             l_w[s, h] = load(w_hbm.at[:, pl.ds(col, H)], w.at[s, h])
-    l_tok = load(tok_hbm, tok)
-
+
+    load_w(7)
     for cp in l_att:
         cp.wait()
     mine = pl.ds(pl.multiple_of(T * (1 - c), T), T)
@@ -133,6 +134,9 @@
     for i in range(2):
         at[i, :, mine] = nt(perm[i], a_own[...]).astype(BF16)
         a_swap.append(send(at.at[i, :, mine], at.at[i, :, mine], co))
+    for s in (4, 5, 0, 1, 6, 3, 2):
+        load_w(s)
+    l_tok = load(tok_hbm, tok)
 
     x1, x2, zf, zn, zt, r1 = {}, {}, {}, {}, {}, {}
     xf, xn, xl = (x + 2) % 4, (x + 1) % 4, (x + 3) % 4

time: 68.3 us -> 68.3 us (level)
  no operation moved by 1% of the time
where the time goes in v6:
time: 68.3 us; the launch traced here: 68.2 us
  Pallas kernels  65.3 us (96%)
  local copies, waits for them, and re-layouts  2.31 us (3%)
    pallas_call x1, Pallas kernels, body(): pl.pallas_call(functools.partial(kernel, factor), out_shape=(vm((T, E), B...  65.3 us
    unnamed x3, local copies, waits for them, and re-layouts  2.31 us

profile of v6, /device:TPU:1, one launch (start us, length us, event | category | flops | bytes accessed | tf_op | source)
XLA Modules:
  0.0 68.2 jit_solution(4178497547566205692)
XLA Ops:
  0.6 65.3 %shard_map.67 = (bf16[256,768]{1,0:T(8,128)(2,1)S(1)}, bf16[6,256,128]{2,1,0:T(8,128)(2,1)S(1)}, f32[6,4,6144]{2,1,0:T(4,128)S(1)}) custom-call(bf16[256,768]{1,0:T(8,128)(2,1)} %tok_hbm.1, bf16[6,256,128]{2,1,0:T(8,128)(2,1)} %bitcast.9, bf16[768,6144]{1,0:T(8,128)(2,1)} %bitcast.8, bf16[256,768]{1,0:T(8,128)(2,1)} %cot_hbm.1), custom_call_target="tpu_custom_call" | custom-call | tf_op jit(solution)/shard_map/pallas_call | solution.py:456
  65.9 0.7 %copy.10 = bf16[256,768]{1,0:T(8,128)(2,1)} copy(bf16[256,768]{1,0:T(8,128)(2,1)S(1)} %get-tuple-element.9) | data formatting | bytes 786432
  66.7 0.7 %copy.11 = bf16[256,6,128]{2,0,1:T(8,128)(2,1)} copy(bf16[256,6,128]{2,0,1:T(8,128)(2,1)S(1)} %bitcast.7) | data formatting | bytes 786432
  67.4 0.8 %copy.12 = f32[4,6,6144]{2,0,1:T(4,128)} copy(f32[4,6,6144]{2,0,1:T(4,128)S(1)} %bitcast.6) | data formatting | bytes 1179648
